TPU v7x, 256 devices: a whole 4x4x8 slice. The times are simulated.
256 devices in a mesh: dp: 16 (over y, x), mem: 16 (over z, core).
Axes of the slice: x: 4, y: 4, z: 8, core: 2. Of those that a mesh axis runs over, the one named last changes fastest.
Arguments:
- tokens: bfloat16 [131072, 2048], P(('dp', 'mem')), may hold values from -320 to 320
- q_weight: bfloat16 [2048, 1024], replicated, may hold values from -0.13 to 0.13
- memory_keys: bfloat16 [16, 64, 128, 512], P('dp', 'mem'), may hold values from -45 to 45
- memory_values: bfloat16 [16, 64, 128, 512], P('dp', 'mem'), may hold values from -6 to 6
- retrieved_block_index: int32 [16, 16, 8], P('dp', 'mem'), may hold values from 0 to 63, as said below
- d_context: bfloat16 [131072, 1024], P(('dp', 'mem')), may hold values from -6 to 6
Outputs:
- context: bfloat16 [131072, 1024], P(('dp', 'mem'))
- grad_tokens: bfloat16 [131072, 2048], P(('dp', 'mem'))
- grad_q_weight: float32 [2048, 1024], P(('dp', 'mem'))
Inputs may be any that keep to these rules, and one draw needn't show every extreme that they name: `retrieved_block_index`: A segment's 8 ids are distinct; at most 2 of them lie in one memory shard (ids k * 4 to (k + 1) * 4 - 1), and in every segment exactly three shards hold 2 of them.
All inputs are finite; a program needn't handle non-finite values.
Results may differ from a plain program's by a relative error of at most 0.015.
Values may be sent and summed in bfloat16 or wider, within the bound.
A program may use at most 128 MiB of HBM per device.

v0:
```python
import functools
import math
import types

import jax
import jax.numpy as jnp
from jax import lax
from jax.experimental import pallas as pl
from jax.experimental.pallas import tpu as pltpu
from jax.sharding import PartitionSpec as P

KVH = 4
HD = 128
TOPB = 8
SEG = 512
D = 2048
QW = 1024
NZ = 8
NMEM = 16
NDP = 16
BLK = 4
CHIP = 2 * BLK
ROWS = 256
SLOTS = 17
LAG = 3
SCALE = 1.0 / HD**0.5
EXP2_SCALE = SCALE * math.log2(math.e)
MESH = pl.DeviceIdType.MESH
F32 = jnp.float32
BF16 = jnp.bfloat16
I32 = jnp.int32


def dot(a, b):
    return jnp.dot(a, b, preferred_element_type=F32)


def scratch(wanted):
    vmem, dma = pltpu.VMEM, pltpu.SemaphoreType.DMA
    table = dict(
        tok=vmem((SEG, D), BF16),
        qw=vmem((D, QW), BF16),
        dctx=vmem((SEG, QW), BF16),
        tok_t=vmem((D, SEG), BF16),
        qw_t=vmem((QW, D), BF16),
        q=vmem((KVH, SEG, 256), BF16),
        dq=vmem((KVH, SEG, 256), BF16),
        k_sel=vmem((TOPB * 128, HD), BF16),
        k_t=vmem((HD, TOPB * 128), BF16),
        v_one=vmem((TOPB * 128, 2 * HD), BF16),
        v_t=vmem((HD, TOPB * 128), BF16),
        g_keep=vmem((D, HD), F32),
        g_send=vmem((KVH, D, HD), BF16),
        g_recv=vmem((KVH, D, HD), BF16),
        g_sum=vmem((KVH, D, HD), BF16),
        dp_recv=vmem((KVH, NDP - 1, 128, HD), BF16),
        in_sem=dma((3,)),
        own_sem=dma((KVH, 2)),
        sib_send=dma((KVH,)),
        sib_recv=dma((KVH,)),
        pair_send=dma((KVH,)),
        pair_recv=dma((KVH,)),
        dp_send=dma((KVH,)),
        dp_rsem=dma((KVH,)),
        z_send=dma((2,)),
        z_rsem=dma((2,)),
    )
    table.update(wanted)
    return table


def slow_scratch():
    vmem, dma = pltpu.VMEM, pltpu.SemaphoreType.DMA
    wanted = dict(
        kv=vmem((KVH, 2, NMEM * BLK, 128, HD), BF16),
        za_send=vmem((NMEM, 8, 4 * HD), F32),
        za_recv=vmem((NMEM - 1, 8, 4 * HD), F32),
        ring_send=dma((KVH, 2)),
        ring_recv=dma((KVH, 2, 2, 4)),
    )
    return scratch(wanted)


def fast_scratch():
    vmem, dma = pltpu.VMEM, pltpu.SemaphoreType.DMA
    wanted = {}
    for h in range(KVH):
        wanted["pool%d" % h] = vmem((CHIP + SLOTS, 2, 128, HD), BF16)
        wanted["oth%d" % h] = vmem((SLOTS, 2, 128, HD), BF16)
        wanted["rcv%d" % h] = vmem((SLOTS, 2, 128, HD), BF16)
        wanted["stg%d" % h] = vmem((SLOTS, 2, 128, HD), BF16)
    wanted.update(
        za_send=vmem((NMEM, 8, 3 * HD), F32),
        za_recv=vmem((NMEM - 1, 8, 3 * HD), F32),
        zb_send=vmem((NMEM, 8, HD), F32),
        zb_recv=vmem((NMEM - 1, 8, HD), F32),
        idx_own=vmem((8, 128), I32),
        idx_all=vmem((NMEM, 8, 128), I32),
        work=vmem((8, 128), I32),
        tab=pltpu.SMEM((8, 128), I32),
        first_work=vmem((8, 128), I32),
        first_tab=pltpu.SMEM((8, 128), I32),
        flag_own=vmem((8, 128), I32),
        flag_all=vmem((NDP - 1, 8, 128), I32),
        chip_send=dma((KVH,)),
        chip_recv=dma((KVH,)),
        hop_send=dma((KVH,)),
        hop_recv=dma((KVH, SLOTS)),
        misc=dma((6,)),
    )
    return scratch(wanted)


def kernel(fast, *refs):
    tok_hbm, qw_hbm, mk_hbm, mv_hbm, idx, dctx_hbm = refs[:6]
    n_out = 4 if fast else 3
    ctx, gt, gw = refs[6:9]
    names = fast_scratch() if fast else slow_scratch()
    v = types.SimpleNamespace(**dict(zip(names, refs[6 + n_out:])))
    dp = lax.axis_index("dp")
    mem = lax.axis_index("mem")
    z = lax.div(mem, 2)
    core = lax.rem(mem, 2)

    def at_z(step):
        return lax.rem(z + step + NZ, NZ) * 2 + core

    def dev(m):
        return (dp, m)

    sib = dev(z * 2 + 1 - core)

    def shard(m):
        return pl.ds(pl.multiple_of(m * BLK, BLK), BLK)

    def remote(src, dst, send_sem, recv_sem, device):
        return pltpu.make_async_remote_copy(
            src_ref=src, dst_ref=dst, send_sem=send_sem, recv_sem=recv_sem,
            device_id=device, device_id_type=MESH,
        )

    def whole(ref, send_sem, recv_sem):
        return remote(ref, ref, send_sem, recv_sem, sib)

    def mem_peers(send):
        def body(j, carry):
            send(j, lax.rem(mem + j, NMEM))
            return carry

        lax.fori_loop(1, NMEM, body, 0)

    def dp_peers(send):
        def body(j, carry):
            send(j, lax.rem(dp + j, NDP))
            return carry

        lax.fori_loop(1, NDP, body, 0)

    if fast:
        pool = (v.pool0, v.pool1, v.pool2, v.pool3)
        oth = (v.oth0, v.oth1, v.oth2, v.oth3)
        rcv = (v.rcv0, v.rcv1, v.rcv2, v.rcv3)
        stg = (v.stg0, v.stg1, v.stg2, v.stg3)
        mine = pl.ds(pl.multiple_of(core * BLK, BLK), BLK)
        own_place = [[pool[h].at[mine, t] for t in range(2)] for h in range(KVH)]
    else:
        kv = v.kv
        own_place = [[kv.at[h, t, shard(mem)] for t in range(2)] for h in range(KVH)]

    loads = [
        pltpu.make_async_copy(tok_hbm, v.tok, v.in_sem.at[0]),
        pltpu.make_async_copy(qw_hbm, v.qw, v.in_sem.at[1]),
        pltpu.make_async_copy(dctx_hbm, v.dctx, v.in_sem.at[2]),
    ]
    own = [
        [
            pltpu.make_async_copy(
                src.at[0, :, :, pl.ds(h * HD, HD)], own_place[h][t], v.own_sem.at[h, t]
            )
            for t, src in enumerate((mk_hbm, mv_hbm))
        ]
        for h in range(KVH)
    ]
    for h in range(KVH):
        for c in own[h]:
            c.start()
    for c in loads:
        c.start()

    barrier = pltpu.get_barrier_semaphore()

    def greet(j, carry):
        pl.semaphore_signal(
            barrier, inc=1, device_id=dev(lax.rem(mem + j, NMEM)), device_id_type=MESH
        )
        pl.semaphore_signal(
            barrier, inc=1, device_id=(lax.rem(dp + j, NDP), mem), device_id_type=MESH
        )
        return carry

    lax.fori_loop(1, NMEM, greet, 0)
    if fast:
        for j in range(TOPB):
            v.idx_own[pl.ds(j, 1), :] = jnp.full((1, 128), idx[0, 0, j], I32)
    pl.semaphore_wait(barrier, 2 * (NMEM - 1))

    def at(n, size):
        return pl.ds(pl.multiple_of(n * size, size), size)

    def project(n):
        v.q[n] = dot(v.tok[...], v.qw[:, at(n, 256)]).astype(BF16)

    def transposes(n):
        v.tok_t[at(n, 512), :] = v.tok[:, at(n, 512)].T
        v.qw_t[:, at(n, 512)] = v.qw[at(n, 512), :].T

    def ready():
        loads[2].wait()
        v.v_one[:, pl.ds(HD, HD)] = jnp.ones((TOPB * 128, HD), BF16)

    def place(j, kb, vb):
        rows = pl.ds(j * 128, 128)
        v.k_sel[rows, :] = kb
        v.k_t[:, rows] = kb.T
        v.v_one[rows, pl.ds(0, HD)] = vb
        v.v_t[:, rows] = vb.T

    def attend(h, j, r):
        rows = at(r, ROWS)
        sub = at(j, HD)
        full = at(2 * h + j, HD)
        do = v.dctx[rows, full]
        s = dot(v.q[h, rows, sub], v.k_t[...])
        top = jnp.max(s, axis=-1, keepdims=True)
        e = jnp.exp2((s - top) * EXP2_SCALE)
        pv = dot(e.astype(BF16), v.v_one[...])
        inv = 1.0 / pv[:, HD:]
        c = pv[:, :HD] * inv
        ctx[rows, full] = c.astype(BF16)
        d_p = dot(do, v.v_t[...])
        delta = jnp.sum(do.astype(F32) * c, axis=-1, keepdims=True)
        ds = (e * (d_p - delta)).astype(BF16)
        v.dq[h, rows, sub] = (dot(ds, v.k_sel[...]) * (inv * SCALE)).astype(BF16)

    def weight_grad(h, first):
        j = 1 - core if first else core
        sub = pl.ds(pl.multiple_of(j * HD, HD), HD)

        def tile(i, carry):
            rows = pl.ds(pl.multiple_of(i * 1024, 1024), 1024)
            g = dot(v.tok_t[rows, :], v.dq[h, :, sub])
            if first:
                v.g_send[h, rows, :] = g.astype(BF16)
            else:
                v.g_keep[rows, :] = g
            return carry

        lax.fori_loop(0, D // 1024, tile, 0)
        if first:
            pair(h).start()

    def part(h, n):
        attend(h, 1 - core if n < 2 else core, n % 2)
        if n % 2 == 1:
            weight_grad(h, n < 2)

    def pair(h):
        return remote(v.g_send.at[h], v.g_recv.at[h], v.pair_send.at[h], v.pair_recv.at[h], sib)

    def dp_start(h):
        pair(h).wait_recv()

        def tile(i, carry):
            rows = pl.ds(pl.multiple_of(i * 256, 256), 256)
            total = v.g_keep[rows, :] + v.g_recv[h, rows, :].astype(F32)
            v.g_sum[h, rows, :] = total.astype(BF16)
            return carry

        lax.fori_loop(0, D // 256, tile, 0)

        def send(j, d):
            rows = pl.ds(pl.multiple_of(d * 128, 128), 128)
            remote(
                v.g_sum.at[h, rows], v.dp_recv.at[h, j - 1], v.dp_send.at[h], v.dp_rsem.at[h],
                (d, mem),
            ).start()

        dp_peers(send)

    def dp_all(h):
        return whole(v.dp_recv.at[h], v.dp_send.at[h], v.dp_rsem.at[h])

    def dp_finish(h, dst, n):
        dp_all(h).wait_recv()
        acc = v.g_sum[h, at(dp, 128), :].astype(F32)
        for j in range(NDP - 1):
            acc = acc + v.dp_recv[h, j].astype(F32)
        dst[:, :, at(n, HD)] = acc.reshape(NMEM, 8, HD)

    def z_start(n, src, dst):
        def send(j, m):
            remote(src.at[m], dst.at[j - 1], v.z_send.at[n], v.z_rsem.at[n], dev(m)).start()

        mem_peers(send)

    def z_all(n, dst):
        return whole(dst, v.z_send.at[n], v.z_rsem.at[n])

    def z_finish(n, src, dst, heads):
        z_all(n, dst).wait_recv()
        same = src[mem]
        other = dst[0]
        for j in range(2, NMEM):
            if j % 2 == 0:
                same = same + dst[j - 1]
            else:
                other = other + dst[j - 1]
        for i, h in enumerate(heads):
            cut = slice(i * HD, (i + 1) * HD)
            gw[:, pl.ds(pl.multiple_of(h * 256 + core * HD, HD), HD)] = same[:, cut]
            gw[:, pl.ds(pl.multiple_of(h * 256 + (1 - core) * HD, HD), HD)] = other[:, cut]

    def grad_tokens():
        def tile(n, carry):
            cols = at(n, 512)
            acc = dot(v.dq[0], v.qw_t[pl.ds(0, 256), cols])
            for h in range(1, KVH):
                acc = acc + dot(v.dq[h], v.qw_t[pl.ds(h * 256, 256), cols])
            gt[:, cols] = acc.astype(BF16)
            return carry

        lax.fori_loop(0, D // 512, tile, 0)

    def each(n, body):
        def run(i, carry):
            body(i)
            return carry

        lax.fori_loop(0, n, run, 0)

    def sent_all():
        for h in range(KVH):
            sib_all(h).wait_send()
            pair(h).wait_send()
            dp_all(h).wait_send()
        z_all(0, v.za_recv).wait_send()

    if not fast:
        def ring(h, t, way, step, back):
            sign = 1 if way == 0 else -1
            piece = kv.at[h, t, shard(at_z(-sign * back))]
            return remote(
                piece, piece, v.ring_send.at[h, t], v.ring_recv.at[h, t, way, step - 1],
                dev(at_z(sign)),
            )

        def to_sib(h, m):
            piece = kv.at[h, :, shard(m)]
            remote(piece, piece, v.sib_send.at[h], v.sib_recv.at[h], sib).start()

        def sib_all(h):
            return whole(kv.at[h, :, pl.ds(0, NZ * BLK)], v.sib_send.at[h], v.sib_recv.at[h])

        def send_own(h):
            for t in range(2):
                for way in range(2):
                    ring(h, t, way, 1, 0).start()
            to_sib(h, mem)

        def ring_step(h, step):
            for t in range(2):
                for way in range(2):
                    if step < 4 or t == way:
                        ring(h, t, way, step, step).wait_recv()
                        if step < 3 or (step == 3 and t == way):
                            ring(h, t, way, step + 1, step).start()
            to_sib(h, at_z(-step))
            if step < 4:
                to_sib(h, at_z(step))

        def head(h):
            for j in range(TOPB):
                b = idx[0, 0, j]
                place(j, kv[h, 0, b], kv[h, 1, b])

            def quarter(n):
                attend(h, lax.rem(1 - core + lax.div(n, 2), 2), lax.rem(n, 2))

            each(4, quarter)
            weight_grad(h, True)
            weight_grad(h, False)
            dp_start(h)
            dp_finish(h, v.za_send, h)

        for h in range(KVH):
            for c in own[h]:
                c.wait()
        each(KVH, send_own)
        for step in range(1, 5):
            each(KVH, functools.partial(ring_step, step=step))
        loads[0].wait()
        loads[1].wait()
        each(KVH, project)
        each(KVH, transposes)
        ready()
        for h in range(KVH):
            sib_all(h).wait_recv()
        each(KVH, head)
        z_start(0, v.za_send, v.za_recv)
        grad_tokens()
        z_finish(0, v.za_send, v.za_recv, (0, 1, 2, 3))
        sent_all()
        for h in range(KVH):
            for t in range(2):
                sent = kv.at[h, t, pl.ds(0, 7 * BLK)]
                whole(sent, v.ring_send.at[h, t], v.ring_recv.at[h, t, 0, 0]).wait_send()
        return

    flag = refs[9]

    def send_idx(j, m):
        remote(v.idx_own, v.idx_all.at[mem], v.misc.at[0], v.misc.at[1], dev(m)).start()

    mem_peers(send_idx)
    v.idx_all[mem] = v.idx_own[...]
    idx_seen = whole(v.idx_all.at[pl.ds(0, NMEM - 1)], v.misc.at[0], v.misc.at[1])

    def chip_copy(h):
        return remote(pool[h].at[mine], pool[h].at[mine], v.chip_send.at[h], v.chip_recv.at[h], sib)

    for h in range(KVH):
        for c in own[h]:
            c.wait()
        chip_copy(h).start()
    loads[0].wait()
    loads[1].wait()
    project(0)
    project(1)
    idx_seen.wait_recv()

    lane1 = lax.broadcasted_iota(I32, (1, 128), 1)
    home1 = lax.shift_right_logical(lane1, 3)
    lane = lax.broadcasted_iota(I32, (8, 128), 1)
    row = lax.broadcasted_iota(I32, (8, 128), 0)
    home = lax.shift_right_logical(lane, 3)
    up = jnp.zeros((1, 128), I32)
    down = jnp.zeros((1, 128), I32)
    far = jnp.zeros((1, 128), I32)
    for c in range(NZ):
        hit = jnp.maximum(
            jnp.where(v.idx_all[2 * c] == lane, 1, 0), jnp.where(v.idx_all[2 * c + 1] == lane, 1, 0)
        )
        hit = jnp.max(hit, axis=0, keepdims=True)
        d = (c - home1 + 16) & 7
        up = jnp.maximum(up, jnp.where((d >= 1) & (d <= 3), d * hit, 0))
        down = jnp.maximum(down, jnp.where(d >= 5, (8 - d) * hit, 0))
        far = jnp.maximum(far, jnp.where(d == 4, hit, 0))

    def load(reach, d):
        return jnp.sum(jnp.where(d < reach, 1, 0), axis=1, keepdims=True)

    def worst(load_of, reach, d):
        return jnp.max(jnp.where((d >= reach) & (d < 4), load_of, 0), axis=0, keepdims=True)

    d_up = (row - home + 16) & 7
    d_down = (home - row + 16) & 7
    up3, down3 = up, down
    for k in range(4):
        cost_up = 4 * worst(load(up, d_up), up3, d_up) + 3 - up3
        cost_down = 4 * worst(load(down, d_down), down3, d_down) + 3 - down3
        upward = (cost_up < cost_down) | ((cost_up == cost_down) & ((lane1 & 4) == 0))
        lot = (far > 0) & ((lane1 & 3) == k)
        up = jnp.where(lot & upward, 4, up)
        down = jnp.where(lot & jnp.logical_not(upward), 4, down)

    def follow(reach, d):
        rem = reach - d
        key = jnp.where(rem > 0, rem * 128 + 127 - lane, 0)
        since = jnp.where(d == 0, 0, 99)
        loc = jnp.where(d == 0, lane & (CHIP - 1), 0)
        sel = jnp.zeros((8, 128), I32)
        return [key, since, loc, sel]

    def step(state, t):
        key, since, loc, sel = state
        k = jnp.where(since <= t, key, 0)
        best = jnp.max(k, axis=1, keepdims=True)
        pick = (k == best) & (k > 0)
        key = jnp.where(pick, 0, key)
        sel = jnp.where(lane == t, jnp.max(jnp.where(pick, loc, 0), axis=1, keepdims=True), sel)
        come = pltpu.roll(jnp.where(pick, 1, 0), 1, 0) > 0
        since = jnp.where(come, t + LAG, since)
        loc = jnp.where(come, CHIP + t, loc)
        return [key, since, loc, sel]

    rings = [follow(up, d_up), follow(down, (row + home) & 7)]
    rev = lax.rem(NZ - z, NZ)

    def pick_row(x, r):
        return jnp.sum(jnp.where(row == r, x, 0), axis=0, keepdims=True)

    onward = dev(lax.rem(z + 1 - 2 * core + NZ, NZ) * 2 + core)

    def hop(h, t):
        return remote(
            stg[h].at[t], rcv[h].at[t], v.hop_send.at[h], v.hop_recv.at[h, t], onward
        )

    def sib_all(h):
        return whole(oth[h], v.sib_send.at[h], v.sib_recv.at[h])

    def take(h, t):
        hop(h, t).wait_recv()
        remote(rcv[h].at[t], oth[h].at[t], v.sib_send.at[h], v.sib_recv.at[h], sib).start()
        pool[h][CHIP + t] = rcv[h][t]

    def round_of(h, t):
        if t == 0:
            chip_copy(h).wait_recv()
        if t >= LAG:
            take(h, t - LAG)
        chosen = v.first_tab[0, t] if h == 0 and t < LAG else v.tab[1, t]
        stg[h][t] = pool[h][chosen]
        hop(h, t).start()

    for t in range(LAG):
        rings = [step(s, t) for s in rings]

    def my_picks():
        picks = jnp.where(core == 0, pick_row(rings[0][3], z), pick_row(rings[1][3], rev))
        return jnp.broadcast_to(picks, (8, 128))

    v.first_work[...] = my_picks()
    to_first = pltpu.make_async_copy(v.first_work, v.first_tab, v.misc.at[5])
    to_first.start()
    to_first.wait()
    for t in range(LAG):
        round_of(0, t)
    for t in range(LAG, SLOTS):
        rings = [step(s, t) for s in rings]
    over = jnp.maximum(rings[0][0], rings[1][0])
    over = jnp.max(jnp.max(over, axis=1, keepdims=True), axis=0, keepdims=True)
    v.flag_own[...] = jnp.broadcast_to(over, (8, 128))

    here = (z - home1 + 16) & 7
    loc_up = pick_row(rings[0][2], z)
    loc_down = pick_row(rings[1][2], rev)
    code = jnp.where(
        here == 0,
        lane1 & (CHIP - 1),
        jnp.where(here <= up, loc_up + SLOTS * core, loc_down + SLOTS * (1 - core)),
    )
    v.work[...] = my_picks()
    v.work[pl.ds(0, 1), :] = code
    to_scalars = pltpu.make_async_copy(v.work, v.tab, v.misc.at[2])
    to_scalars.start()

    def send_flag(j, d):
        remote(v.flag_own, v.flag_all.at[j - 1], v.misc.at[3], v.misc.at[4], (d, mem)).start()

    dp_peers(send_flag)
    to_scalars.wait()

    def prepare(h):
        sib_all(h).wait_recv()
        for j in range(TOPB):
            spot = v.tab[0, idx[0, 0, j]]
            here_kv = pool[h][jnp.minimum(spot, CHIP + SLOTS - 1)]
            there_kv = oth[h][jnp.clip(spot - CHIP - SLOTS, 0, SLOTS - 1)]
            both = jnp.where(spot < CHIP + SLOTS, here_kv, there_kv)
            place(j, both[0], both[1])

    half = SLOTS // 2
    order = [(0, t) for t in range(LAG, half)]
    for h in range(KVH):
        for i in range(SLOTS - half):
            order.append((h, half + i))
            if h + 1 < KVH and i < half:
                order.append((h + 1, i))
    work = [functools.partial(project, 2), functools.partial(project, 3)]
    work += [functools.partial(transposes, n) for n in range(4)] + [ready]
    due = {}
    for n, (h, t) in enumerate(order):
        if t == SLOTS - 1 and h < KVH - 1:
            for i in range(LAG):
                due.setdefault(n + 1 + i, []).append(functools.partial(take, h, SLOTS - LAG + i))
            chunks = [functools.partial(prepare, h)]
            chunks += [functools.partial(part, h, i) for i in range(4)]
            chunks += [functools.partial(dp_start, h)]
            if h == 2:
                chunks += [functools.partial(dp_finish, 0, v.za_send, 0)]
            due.setdefault(n + (5 if h == 2 else 6), []).append(functools.partial(work.extend, chunks))
    for n, (h, t) in enumerate(order):
        round_of(h, t)
        for action in due.pop(n, []):
            action()
        if work and (n % 2 == 1 or n < half or h == 3 and t >= half):
            work.pop(0)()
    for t in range(SLOTS - LAG, SLOTS):
        if work:
            work.pop(0)()
        take(3, t)
    for n in sorted(due):
        for action in due[n]:
            action()
    while work:
        work.pop(0)()
    prepare(3)
    for n in range(4):
        part(3, n)
    dp_start(3)
    dp_finish(1, v.za_send, 1)
    dp_finish(2, v.za_send, 2)
    z_start(0, v.za_send, v.za_recv)
    grad_tokens()
    z_finish(0, v.za_send, v.za_recv, (0, 1, 2))
    dp_finish(3, v.zb_send, 0)
    z_start(1, v.zb_send, v.zb_recv)
    z_finish(1, v.zb_send, v.zb_recv, (3,))
    sent_all()
    z_all(1, v.zb_recv).wait_send()
    dp_seen = whole(v.flag_all, v.misc.at[3], v.misc.at[4])
    dp_seen.wait_recv()
    flag[...] = jnp.maximum(v.flag_own[...], jnp.max(v.flag_all[...], axis=0))
    for h in range(KVH):
        chip_copy(h).wait_send()
        whole(rcv[h], v.hop_send.at[h], v.hop_recv.at[h, 0]).wait_send()
    idx_seen.wait_send()
    dp_seen.wait_send()


def call(fast, args):
    hbm = pl.BlockSpec(memory_space=pl.ANY)
    vmem = pltpu.VMEM
    outs = [
        vmem((SEG, QW), BF16),
        vmem((SEG, D), BF16),
        vmem((D // (NDP * NMEM), QW), F32),
    ]
    if fast:
        outs.append(vmem((8, 128), I32))
    return pl.pallas_call(
        functools.partial(kernel, fast),
        out_shape=outs,
        in_specs=[hbm, hbm, hbm, hbm, pl.BlockSpec(memory_space=pltpu.SMEM), hbm],
        out_specs=[pl.BlockSpec(memory_space=vmem)] * len(outs),
        scratch_shapes=list((fast_scratch() if fast else slow_scratch()).values()),
        compiler_params=pltpu.CompilerParams(
            collective_id=0 if fast else 1,
            has_side_effects=True,
            vmem_limit_bytes=(58 if fast else 52) * 1024 * 1024,
        ),
    )(*args)


def store(*refs):
    copies = [
        pltpu.make_async_copy(src, dst, refs[6].at[i])
        for i, (src, dst) in enumerate(zip(refs[:3], refs[3:6]))
    ]
    for c in copies:
        c.start()
    for c in copies:
        c.wait()


def on_device(*args):
    ctx, gt, gw, flag = call(True, args)
    outs = lax.cond(flag[0, 0] > 0, lambda: tuple(call(False, args)), lambda: (ctx, gt, gw))
    hbm = pl.BlockSpec(memory_space=pl.ANY)
    return pl.pallas_call(
        store,
        out_shape=[jax.ShapeDtypeStruct(x.shape, x.dtype) for x in outs],
        in_specs=[hbm] * 3,
        out_specs=[hbm] * 3,
        scratch_shapes=[pltpu.SemaphoreType.DMA((3,))],
    )(*outs)


def solution(mesh):
    return jax.shard_map(
        on_device,
        mesh=mesh,
        in_specs=(
            P(("dp", "mem"), None),
            P(),
            P("dp", "mem", None, None),
            P("dp", "mem", None, None),
            P("dp", "mem", None),
            P(("dp", "mem"), None),
        ),
        out_specs=(P(("dp", "mem"), None), P(("dp", "mem"), None), P(("dp", "mem"), None)),
        check_vma=False,
    )
```

profile of v0, /device:TPU:1, one launch (start us, length us, event | category | flops | bytes accessed | tf_op | source)
XLA Modules:
  0.0 106.0 jit_solution(17112700828261231867)
XLA Ops:
  0.6 0.0 copy-start
  0.6 102.3 %shard_map.85 = (bf16[512,1024]{1,0:T(8,128)(2,1)S(1)}, bf16[512,2048]{1,0:T(8,128)(2,1)S(1)}, f32[8,1024]{1,0:T(8,128)S(1)}, s32[8,128]{1,0:T(8,128)S(1)}) custom-call(bf16[512,2048]{1,0:T(8,128)(2,1)} %refs_0_.1, bf16[2048,1024]{1,0:T(8,128)(2,1)} %refs_1_.1, bf16[1,4,128,512]{3,2,1,0:T(8,128)(2,1)} %refs_2_.1, bf16[1,4,128,512]{3,2,1,0:T(8,128)(2,1)} %refs_3_.1, ...), custom_call_target="tpu_custom_call" | custom-call | tf_op jit(solution)/shard_map/pallas_call | solution.py:642
  102.9 0.5 slice.3
  104.1 0.0 copy-done
  104.1 1.7 %shard_map.86 = (bf16[512,1024]{1,0:T(8,128)(2,1)}, bf16[512,2048]{1,0:T(8,128)(2,1)}, f32[8,1024]{1,0:T(8,128)}) custom-call(bf16[512,1024]{1,0:T(8,128)(2,1)S(1)} %get-tuple-element.38.refs_0_, bf16[512,2048]{1,0:T(8,128)(2,1)S(1)} %get-tuple-element.39.refs_1_, f32[8,1024]{1,0:T(8,128)S(1)} %get-tuple-element.40.refs_2_), custom_call_target="tpu_custom_call" | custom-call | tf_op jit(solution)/shard_map/pallas_call | solution.py:671
  (1 shorter events, 0.0 us)
Async XLA Ops:
  0.6 103.5 %copy-start = (s32[1,1,8]{2,1,0:T(1,128)S(1)}, s32[1,1,8]{2,1,0:T(1,128)}, u32[]{:S(2)}) copy-start(s32[1,1,8]{2,1,0:T(1,128)} %refs_4_.1) | copy-start | bytes 100
where the time goes:
time: 106 us
  Pallas kernels  104 us (98%)
  between operations  1.5 us (1%)
    pallas_call x1, Pallas kernels, call(): pl.pallas_call(functools.partial(kernel, fast), out_shape=outs, in_specs=...  102 us

commit v1 on v0

--- a/solution.py
+++ b/solution.py
@@ -270,22 +270,20 @@
     def dp_start(h):
         pair(h).wait_recv()
 
-        def tile(i, carry):
-            rows = pl.ds(pl.multiple_of(i * 256, 256), 256)
+        def add_up(d):
+            rows = at(d, 128)
             total = v.g_keep[rows, :] + v.g_recv[h, rows, :].astype(F32)
             v.g_sum[h, rows, :] = total.astype(BF16)
-            return carry
-
-        lax.fori_loop(0, D // 256, tile, 0)
 
         def send(j, d):
-            rows = pl.ds(pl.multiple_of(d * 128, 128), 128)
+            add_up(d)
             remote(
-                v.g_sum.at[h, rows], v.dp_recv.at[h, j - 1], v.dp_send.at[h], v.dp_rsem.at[h],
+                v.g_sum.at[h, at(d, 128)], v.dp_recv.at[h, j - 1], v.dp_send.at[h], v.dp_rsem.at[h],
                 (d, mem),
             ).start()
 
         dp_peers(send)
+        add_up(dp)
 
     def dp_all(h):
         return whole(v.dp_recv.at[h], v.dp_send.at[h], v.dp_rsem.at[h])
@@ -571,12 +569,20 @@
             place(j, both[0], both[1])
 
     half = SLOTS // 2
-    order = [(0, t) for t in range(LAG, half)]
+    order = []
+    upcoming = [LAG, 0, 0, 0]
+
+    def put(h):
+        if h < KVH and upcoming[h] < SLOTS:
+            order.append((h, upcoming[h]))
+            upcoming[h] += 1
+
+    for h in (0, 0, 1) * 3:
+        put(h)
     for h in range(KVH):
-        for i in range(SLOTS - half):
-            order.append((h, half + i))
-            if h + 1 < KVH and i < half:
-                order.append((h + 1, i))
+        while upcoming[h] < SLOTS:
+            put(h)
+            put(h + 1)
     work = [functools.partial(project, 2), functools.partial(project, 3)]
     work += [functools.partial(transposes, n) for n in range(4)] + [ready]
     due = {}

time: 106 us -> 106 us (level)
  no operation moved by 1% of the time
where the time goes in v1:
time: 106 us
  Pallas kernels  104 us (98%)
  between operations  1.5 us (1%)
    pallas_call x1, Pallas kernels, call(): pl.pallas_call(functools.partial(kernel, fast), out_shape=outs, in_specs=...  102 us

profile of v1, /device:TPU:1, one launch (start us, length us, event | category | flops | bytes accessed | tf_op | source)
XLA Modules:
  0.0 106.1 jit_solution(246223130799999881)
XLA Ops:
  0.6 0.0 copy-start
  0.6 102.4 %shard_map.85 = (bf16[512,1024]{1,0:T(8,128)(2,1)S(1)}, bf16[512,2048]{1,0:T(8,128)(2,1)S(1)}, f32[8,1024]{1,0:T(8,128)S(1)}, s32[8,128]{1,0:T(8,128)S(1)}) custom-call(bf16[512,2048]{1,0:T(8,128)(2,1)} %refs_0_.1, bf16[2048,1024]{1,0:T(8,128)(2,1)} %refs_1_.1, bf16[1,4,128,512]{3,2,1,0:T(8,128)(2,1)} %refs_2_.1, bf16[1,4,128,512]{3,2,1,0:T(8,128)(2,1)} %refs_3_.1, ...), custom_call_target="tpu_custom_call" | custom-call | tf_op jit(solution)/shard_map/pallas_call | solution.py:648
  103.0 0.5 slice.3
  104.2 0.0 copy-done
  104.2 1.7 %shard_map.86 = (bf16[512,1024]{1,0:T(8,128)(2,1)}, bf16[512,2048]{1,0:T(8,128)(2,1)}, f32[8,1024]{1,0:T(8,128)}) custom-call(bf16[512,1024]{1,0:T(8,128)(2,1)S(1)} %get-tuple-element.38.refs_0_, bf16[512,2048]{1,0:T(8,128)(2,1)S(1)} %get-tuple-element.39.refs_1_, f32[8,1024]{1,0:T(8,128)S(1)} %get-tuple-element.40.refs_2_), custom_call_target="tpu_custom_call" | custom-call | tf_op jit(solution)/shard_map/pallas_call | solution.py:677
  (1 shorter events, 0.0 us)
Async XLA Ops:
  0.6 103.6 %copy-start = (s32[1,1,8]{2,1,0:T(1,128)S(1)}, s32[1,1,8]{2,1,0:T(1,128)}, u32[]{:S(2)}) copy-start(s32[1,1,8]{2,1,0:T(1,128)} %refs_4_.1) | copy-start | bytes 100
